TPU v7x, 32 devices: a whole 2x2x4 slice. The times are simulated.
32 devices in a mesh: tm: 4 (over y, x), pts: 8 (over z, core).
Axes of the slice: x: 2, y: 2, z: 4, core: 2. Of those that a mesh axis runs over, the one named last changes fastest.
Arguments:
- series: bfloat16 [8192, 3, 8192], P('tm', None, 'pts'), may hold values from -6 to 6
- weights: float32 [8192], P('pts'), may hold values from 1.2207031e-05 to 0.00012207031
- freq_bins: int32 [16], replicated, may hold values from 1 to 255
Outputs:
- cross_gram: float32 [16, 2, 32, 32], P('tm')
- spatial_modes: bfloat16 [16, 2, 32, 3, 8192], P('tm', None, None, None, 'pts')
All inputs are finite; a program needn't handle non-finite values.
Results may differ from a plain program's by a relative error of at most 0.0067.
Values may be sent and summed in bfloat16 or wider, within the bound.
A program may use at most 128 MiB of HBM per device.

v0:
```python
import jax
import jax.numpy as jnp
from jax import lax
from jax.sharding import PartitionSpec as P

NFFT = 512
NB = 32
NF = 16
ITERS = 4


def from_behind(block, axis, distance):
    devices = range(lax.axis_size(axis))
    route = [((i - distance) % len(devices), i) for i in devices]
    return lax.ppermute(block, axis, route)


def build_table(freq_bins):
    sample_index = jnp.arange(NFFT, dtype=jnp.int32)
    window = (
        0.5 - 0.5 * jnp.cos(2.0 * jnp.pi * sample_index.astype(jnp.float32) / NFFT)
    ) * jnp.sqrt(8.0 / (3.0 * NFFT))
    product_index = freq_bins[:, None] * sample_index[None, :] % NFFT
    phase_angle = 2.0 * jnp.pi * product_index.astype(jnp.float32) / NFFT
    kernel_table = jnp.stack(
        [jnp.cos(phase_angle) * window, -jnp.sin(phase_angle) * window], axis=1
    )
    return kernel_table.reshape(2 * NF, NFFT).astype(jnp.bfloat16)


def matmul_high(left, right):
    return jnp.matmul(left, right, precision=lax.Precision.HIGHEST)


def combine(pair_gram):
    real_part = pair_gram[..., :NB, :NB] + pair_gram[..., NB:, NB:]
    imag_part = pair_gram[..., :NB, NB:] - pair_gram[..., NB:, :NB]
    return jnp.stack([real_part, imag_part], axis=-3)


def inverse_root(cross_gram):
    real_part = cross_gram[..., 0, :, :]
    imag_part = cross_gram[..., 1, :, :]
    norm_value = jnp.sqrt(jnp.sum(cross_gram * cross_gram, axis=(-3, -2, -1)))
    upper_rows = jnp.concatenate([real_part, -imag_part], axis=-1)
    lower_rows = jnp.concatenate([imag_part, real_part], axis=-1)
    current = jnp.concatenate([upper_rows, lower_rows], axis=-2) / norm_value[..., None, None]
    identity = jnp.eye(2 * NB, dtype=jnp.float32)
    inv_root = jnp.broadcast_to(identity, current.shape)
    for iteration in range(ITERS):
        factor = 0.5 * (3.0 * identity - matmul_high(inv_root, current))
        current = matmul_high(current, factor)
        inv_root = matmul_high(factor, inv_root)
    return inv_root


def on_device(series, weights, freq_bins):
    kernel_table = build_table(freq_bins)
    half_len = NFFT // 2
    point_cols = series.shape[1] * series.shape[2]
    local_blocks = series.shape[0] // half_len
    halves = series.reshape(local_blocks, half_len, point_cols)
    first_half = jnp.einsum(
        "kn,jnp->kjp", kernel_table[:, :half_len], halves, preferred_element_type=jnp.float32
    )
    received = from_behind(series[:half_len], "tm", -1)
    following = jnp.concatenate([halves[1:], received.reshape(1, half_len, point_cols)], axis=0)
    second_half = jnp.einsum(
        "kn,jnp->kjp", kernel_table[:, half_len:], following, preferred_element_type=jnp.float32
    )
    coefficients = (first_half + second_half).astype(jnp.bfloat16)
    regrouped = lax.all_to_all(
        coefficients.reshape(NF, 2, local_blocks, point_cols),
        "tm",
        split_axis=0,
        concat_axis=2,
        tiled=True,
    )
    local_bins = regrouped.shape[0]
    freq_rows = regrouped.reshape(local_bins, 2 * NB, point_cols)
    row_weight = jnp.tile(weights, 3)
    weighted = freq_rows.astype(jnp.float32) * row_weight
    weighted_high = weighted.astype(jnp.bfloat16)
    weighted_low = (weighted - weighted_high.astype(jnp.float32)).astype(jnp.bfloat16)
    pair_gram = jnp.einsum(
        "fip,fjp->fij", weighted_high, freq_rows, preferred_element_type=jnp.float32
    )
    pair_gram = pair_gram + jnp.einsum(
        "fip,fjp->fij", weighted_low, freq_rows, preferred_element_type=jnp.float32
    )
    cross_gram = combine(lax.psum(pair_gram, "pts"))
    inv_root = inverse_root(cross_gram).astype(jnp.bfloat16)
    spatial_modes = jnp.einsum(
        "fij,fjp->fip", inv_root, freq_rows, preferred_element_type=jnp.float32
    ).astype(jnp.bfloat16)
    return (cross_gram, spatial_modes.reshape(local_bins, 2, NB, 3, series.shape[2]))


def solution(mesh):
    in_specs = (P("tm", None, "pts"), P("pts"), P())
    out_specs = (P("tm", None, None, None), P("tm", None, None, None, "pts"))
    return jax.shard_map(
        on_device, mesh=mesh, in_specs=in_specs, out_specs=out_specs, check_vma=False
    )
```

profile of v0, /device:TPU:0, one launch (start us, length us, event | category | flops | bytes accessed | tf_op | source)
XLA Modules:
  0.0 247.0 jit_solution(15785877224248194130)
XLA Ops:
  7.2 1.4 slice-done
  8.6 1.6 copy.54
  10.1 3.9 %collective-permute-start = (bf16[256,3,1024]{0,2,1:T(8,128)(2,1)}, bf16[256,3,1024]{0,2,1:T(8,128)(2,1)}, u32[]{:S(2)}, u32[]{:S(2)}) collective-permute-start(bf16[256,3,1024]{0,2,1:T(8,128)(2,1)} %copy.54), channel_id=1, source_target_pairs={{8,0},{16,8},{24,16},{0,24},{9,1},{17,9},{25,17},{1,25},{10,2},{18... | collective-permute-start | bytes 4718600 | tf_op jit(solution)/shard_map/ppermute | solution.py:15
  14.0 18.8 %copy.50 = bf16[2048,3,1024]{2,1,0:T(4,128)(2,1)} copy(bf16[2048,3,1024]{2,0,1:T(8,128)(2,1)} %param.3) | data formatting | bytes 25165824 | tf_op jit(solution)/shard_map/reshape | solution.py:62
  32.9 10.2 %slice.29 = bf16[1792,3,1024]{2,0,1:T(8,128)(2,1)} slice(bf16[2048,3,1024]{2,0,1:T(8,128)(2,1)} %param.3), slice={[256:2048], [0:3], [0:1024]} | slice | bytes 22020096 | tf_op jit(solution)/shard_map/slice | solution.py:67
  43.4 34.5 %reshape.188 = bf16[8,256,3072]{2,1,0:T(8,128)(2,1)} reshape(bf16[2048,3,1024]{2,1,0:T(4,128)(2,1)} %copy.50) | data formatting | bytes 25165824 | tf_op jit(solution)/shard_map/reshape | solution.py:62
  77.9 16.8 %copy.51 = bf16[1792,3,1024]{2,1,0:T(4,128)(2,1)} copy(bf16[1792,3,1024]{2,0,1:T(8,128)(2,1)} %slice.29) | data formatting | bytes 22020096 | tf_op jit(solution)/shard_map/slice | solution.py:67
  94.7 30.2 %reshape.189 = bf16[7,256,3072]{2,1,0:T(8,128)(2,1)} reshape(bf16[1792,3,1024]{2,1,0:T(4,128)(2,1)} %copy.51) | data formatting | bytes 22020096 | tf_op jit(solution)/shard_map/slice | solution.py:67
  124.9 6.8 %fusion.32 = f32[32,8,3072]{2,0,1:T(8,128)S(1)} fusion(bf16[8,256,3072]{2,1,0:T(8,128)(2,1)} %reshape.188, bf16[32,512]{1,0:T(8,128)(2,1)S(1)} %convert_element_type.55), kind=kOutput, calls=%fused_computation.49 | convolution fusion | flops 402653184 | bytes 15745024 | tf_op jit(solution)/shard_map/kn,jnp->kjp/dot_general | solution.py:63
  131.7 2.6 %copy.45 = bf16[1,256,3072]{2,1,0:T(8,128)(2,1)} copy(bf16[1,256,3072]{1,2,0:T(8,128)(2,1)} %bitcast.2) | data formatting | bytes 3145728 | tf_op jit(solution)/shard_map/reshape | solution.py:67
  134.3 7.0 %fusion.7 = bf16[32,8,3072]{2,0,1:T(8,128)(2,1)} fusion(f32[32,8,3072]{2,0,1:T(8,128)S(1)} %fusion.32, bf16[1,256,3072]{2,1,0:T(8,128)(2,1)} %copy.45, bf16[7,256,3072]{2,1,0:T(8,128)(2,1)} %reshape.189, bf16[32,512]{1,0:T(8,128)(2,1)S(1)} %convert_element_type.55), kind=kOutput, calls=%fused_computation.5 | convolution fusion | flops 429391872 | bytes 17317888 | tf_op jit(solution)/shard_map/kn,jnp->kjp/dot_general | solution.py:68
  141.3 3.5 %reshape.183 = bf16[16,2,8,3072]{3,1,0,2:T(2,128)(2,1)S(1)} reshape(bf16[32,8,3072]{2,0,1:T(8,128)(2,1)} %fusion.7) | data formatting | bytes 3145728 | tf_op jit(solution)/shard_map/reshape | solution.py:73
  144.9 2.7 %copy.46 = bf16[16,2,8,3072]{3,1,2,0:T(2,128)(2,1)} copy(bf16[16,2,8,3072]{3,1,0,2:T(2,128)(2,1)S(1)} %reshape.183) | data formatting | bytes 3145728 | tf_op jit(solution)/shard_map/reshape | solution.py:73
  147.5 3.6 %all-to-all-start = ((bf16[16,2,8,3072]{3,1,2,0:T(2,128)(2,1)}), bf16[16,2,8,3072]{3,1,2,0:T(2,128)(2,1)S(1)}, u32[]{:S(2)}, u32[]{:S(2)}) async-start(bf16[16,2,8,3072]{3,1,2,0:T(2,128)(2,1)} %copy.46), calls=%async_computation | async-start | bytes 3145728 | tf_op jit(solution)/shard_map/all_to_all | solution.py:72
  151.4 18.9 %all-to-all-done = bf16[16,2,8,3072]{3,1,2,0:T(2,128)(2,1)S(1)} async-done(((bf16[16,2,8,3072]{3,1,2,0:T(2,128)(2,1)}), bf16[16,2,8,3072]{3,1,2,0:T(2,128)(2,1)S(1)}, u32[]{:S(2)}, u32[]{:S(2)}) %all-to-all-start) | async-done | bytes 1572896 | tf_op jit(solution)/shard_map/all_to_all | solution.py:72
  170.3 0.3 copy.47
  170.7 0.6 fusion.11
  171.2 1.3 fusion.16
  172.5 54.7 %all-reduce.2.cloned.1.call-done = f32[4,64,64]{2,1,0:T(8,128)} async-done(((f32[4,64,64]{2,1,0:T(8,128)}), f32[4,64,64]{2,1,0:T(8,128)}) %all-reduce.2.cloned.1.call-update) | async-done | bytes 65552 | tf_op jit(solution)/shard_map/psum | solution.py:91
  227.2 1.0 fusion.35
  228.4 0.4 fusion.20
  228.7 0.3 fusion.34
  229.3 0.3 fusion.19
  229.6 0.3 fusion.37
  230.1 0.3 fusion.18
  230.4 0.3 fusion.39
  230.9 0.3 fusion.17
  231.2 0.3 convolution_convert_fusion.1
  231.4 1.7 convolution_convert_fusion
  233.1 4.6 %reshape.185 = bf16[4,2,32,3,1024]{4,3,2,1,0:T(4,128)(2,1)S(1)} reshape(bf16[4,64,3072]{2,1,0:T(8,128)(2,1)} %convolution_convert_fusion) | data formatting | bytes 3145728 | tf_op jit(solution)/shard_map/reshape | solution.py:96
  237.7 1.8 copy.49
  239.5 0.7 copy.48
  (22 shorter events, 1.5 us)
Async XLA Ops:
  7.2 1.4 slice-start
  10.1 121.6 %collective-permute-start = (bf16[256,3,1024]{0,2,1:T(8,128)(2,1)}, bf16[256,3,1024]{0,2,1:T(8,128)(2,1)}, u32[]{:S(2)}, u32[]{:S(2)}) collective-permute-start(bf16[256,3,1024]{0,2,1:T(8,128)(2,1)} %copy.54), channel_id=1, source_target_pairs={{8,0},{16,8},{24,16},{0,24},{9,1},{17,9},{25,17},{1,25},{10,2},{18... | collective-permute-start | bytes 4718600 | tf_op jit(solution)/shard_map/ppermute | solution.py:15
  32.9 10.3 %copy-start.1 = (s32[16]{0:T(128)S(1)}, s32[16]{0:T(128)}, u32[]{:S(2)}) copy-start(s32[16]{0:T(128)} %param.5) | copy-start | bytes 196
  144.8 6.5 %copy-start = (f32[1024]{0:T(1024)S(1)}, f32[1024]{0:T(1024)}, u32[]{:S(2)}) copy-start(f32[1024]{0:T(1024)} %param.4) | copy-start | bytes 12292
  147.5 22.8 %all-to-all-start = ((bf16[16,2,8,3072]{3,1,2,0:T(2,128)(2,1)}), bf16[16,2,8,3072]{3,1,2,0:T(2,128)(2,1)S(1)}, u32[]{:S(2)}, u32[]{:S(2)}) async-start(bf16[16,2,8,3072]{3,1,2,0:T(2,128)(2,1)} %copy.46), calls=%async_computation | async-start | bytes 3145728 | tf_op jit(solution)/shard_map/all_to_all | solution.py:72
  151.1 76.1 %all-reduce.2.cloned.1.call-start = ((), (), s32[]{:S(2)}) async-start(), calls=%async_computation.1 | async-start | bytes 262144 | tf_op jit(solution)/shard_map/psum | solution.py:91
Sparse Core Ops, SparseCore 0:
  172.6 54.5 all-reduce.1
where the time goes:
time: 249 us; the launch traced here: 247 us
  local copies, waits for them, and re-layouts  130 us (52%)
  waiting for transfers between devices  73.6 us (30%)
  matrix products  20.3 us (8%)
  between operations  14.3 us (6%)
  starting transfers between devices  7.68 us (3%)
    slice x3, local copies, waits for them, and re-layouts, on_device(): halves[1:]  57.2 us
    psum x1, waiting for transfers between devices, on_device(): cross_gram = combine(lax.psum(pair_gram, 'pts'))  54.7 us
    reshape x2, local copies, waits for them, and re-layouts, on_device(): halves = series.reshape(local_blocks, half_len, point_cols)  53.3 us
    all_to_all x1, waiting for transfers between devices, on_device(): lax.all_to_all(coefficients.reshape(NF, 2, local_blocks, point_cols), 'tm...  18.9 us
    dot_general x1, matrix products, on_device(): jnp.einsum('kn,jnp->kjp', kernel_table[:, half_len:], following, preferre...  7.02 us
    dot_general x1, matrix products, on_device(): jnp.einsum('kn,jnp->kjp', kernel_table[:, :half_len], halves, preferred_e...  6.83 us
    reshape x2, local copies, waits for them, and re-layouts, on_device(): coefficients.reshape(NF, 2, local_blocks, point_cols)  6.16 us
  transfers between devices with their start and end apart: 3, of which 2 were waited for; matrix products, arithmetic and copies ran while one was open for 48% of the time, Pallas kernels for 0%

commit v1 on v0

--- a/solution.py
+++ b/solution.py
@@ -88,7 +88,7 @@
     pair_gram = pair_gram + jnp.einsum(
         "fip,fjp->fij", weighted_low, freq_rows, preferred_element_type=jnp.float32
     )
-    cross_gram = combine(lax.psum(pair_gram, "pts"))
+    cross_gram = combine(jnp.sum(lax.all_gather(pair_gram, "pts"), axis=0))
     inv_root = inverse_root(cross_gram).astype(jnp.bfloat16)
     spatial_modes = jnp.einsum(
         "fij,fjp->fip", inv_root, freq_rows, preferred_element_type=jnp.float32

time: 249 us -> 196 us (0.79)
  waiting for transfers between devices: 73.6 us -> 19 us
  blocking collectives: 0 us -> 17 us
  between operations: 14.3 us -> 0.87 us
    psum x1 -> x0, waiting for transfers between devices: 54.7 us -> none  [on_device(): cross_gram = combine(lax.psum(pair_gram, 'pts'))]
    all_gather x0 -> x1, blocking collectives: none -> 17 us  [on_device(): cross_gram = combine(jnp.sum(lax.all_gather(pair_gram, 'pts'), axis=0))]
  transfers between devices with their start and end apart: 3 -> 2, of which waited for: 2 -> 1; matrix products, arithmetic and copies ran while one was open for 48% -> 61% of each run, Pallas kernels for 0% -> 0%
where the time goes in v1:
time: 196 us; the launch traced here: 194 us
  local copies, waits for them, and re-layouts  129 us (66%)
  matrix products  19.7 us (10%)
  waiting for transfers between devices  19 us (10%)
  blocking collectives  17 us (9%)
  starting transfers between devices  7.64 us (4%)
    slice x3, local copies, waits for them, and re-layouts, on_device(): halves[1:]  57.2 us
    reshape x2, local copies, waits for them, and re-layouts, on_device(): halves = series.reshape(local_blocks, half_len, point_cols)  53.3 us
    all_to_all x1, waiting for transfers between devices, on_device(): lax.all_to_all(coefficients.reshape(NF, 2, local_blocks, point_cols), 'tm...  19 us
    all_gather x1, blocking collectives, on_device(): cross_gram = combine(jnp.sum(lax.all_gather(pair_gram, 'pts'), axis=0))  17 us
    dot_general x1, matrix products, on_device(): jnp.einsum('kn,jnp->kjp', kernel_table[:, half_len:], following, preferre...  7.04 us
    dot_general x1, matrix products, on_device(): jnp.einsum('kn,jnp->kjp', kernel_table[:, :half_len], halves, preferred_e...  6.83 us
    reshape x2, local copies, waits for them, and re-layouts, on_device(): coefficients.reshape(NF, 2, local_blocks, point_cols)  6.16 us
    reshape x1, local copies, waits for them, and re-layouts, on_device(): spatial_modes.reshape(local_bins, 2, NB, 3, series.shape[2])  4.59 us
  transfers between devices with their start and end apart: 2, of which 1 were waited for; matrix products, arithmetic and copies ran while one was open for 61% of the time, Pallas kernels for 0%

profile of v1, /device:TPU:0, one launch (start us, length us, event | category | flops | bytes accessed | tf_op | source)
XLA Modules:
  0.0 194.3 jit_solution(6516924732085248386)
XLA Ops:
  0.6 1.4 slice-done
  2.0 1.6 copy.54
  3.6 3.9 %collective-permute-start = (bf16[256,3,1024]{0,2,1:T(8,128)(2,1)}, bf16[256,3,1024]{0,2,1:T(8,128)(2,1)}, u32[]{:S(2)}, u32[]{:S(2)}) collective-permute-start(bf16[256,3,1024]{0,2,1:T(8,128)(2,1)} %copy.54), channel_id=1, source_target_pairs={{8,0},{16,8},{24,16},{0,24},{9,1},{17,9},{25,17},{1,25},{10,2},{18... | collective-permute-start | bytes 4718600 | tf_op jit(solution)/shard_map/ppermute | solution.py:15
  7.5 18.8 %copy.50 = bf16[2048,3,1024]{2,1,0:T(4,128)(2,1)} copy(bf16[2048,3,1024]{2,0,1:T(8,128)(2,1)} %param.3) | data formatting | bytes 25165824 | tf_op jit(solution)/shard_map/reshape | solution.py:62
  26.3 10.2 %slice.29 = bf16[1792,3,1024]{2,0,1:T(8,128)(2,1)} slice(bf16[2048,3,1024]{2,0,1:T(8,128)(2,1)} %param.3), slice={[256:2048], [0:3], [0:1024]} | slice | bytes 22020096 | tf_op jit(solution)/shard_map/slice | solution.py:67
  36.9 34.5 %reshape.189 = bf16[8,256,3072]{2,1,0:T(8,128)(2,1)} reshape(bf16[2048,3,1024]{2,1,0:T(4,128)(2,1)} %copy.50) | data formatting | bytes 25165824 | tf_op jit(solution)/shard_map/reshape | solution.py:62
  71.3 16.7 %copy.51 = bf16[1792,3,1024]{2,1,0:T(4,128)(2,1)} copy(bf16[1792,3,1024]{2,0,1:T(8,128)(2,1)} %slice.29) | data formatting | bytes 22020096 | tf_op jit(solution)/shard_map/slice | solution.py:67
  88.1 30.2 %reshape.190 = bf16[7,256,3072]{2,1,0:T(8,128)(2,1)} reshape(bf16[1792,3,1024]{2,1,0:T(4,128)(2,1)} %copy.51) | data formatting | bytes 22020096 | tf_op jit(solution)/shard_map/slice | solution.py:67
  118.3 6.8 %fusion.32 = f32[32,8,3072]{2,0,1:T(8,128)S(1)} fusion(bf16[8,256,3072]{2,1,0:T(8,128)(2,1)} %reshape.189, bf16[32,512]{1,0:T(8,128)(2,1)S(1)} %convert_element_type.55), kind=kOutput, calls=%fused_computation.49 | convolution fusion | flops 402653184 | bytes 15745024 | tf_op jit(solution)/shard_map/kn,jnp->kjp/dot_general | solution.py:63
  125.2 2.6 %copy.45 = bf16[1,256,3072]{2,1,0:T(8,128)(2,1)} copy(bf16[1,256,3072]{1,2,0:T(8,128)(2,1)} %bitcast.2) | data formatting | bytes 3145728 | tf_op jit(solution)/shard_map/reshape | solution.py:67
  127.7 7.0 %fusion.7 = bf16[32,8,3072]{2,0,1:T(8,128)(2,1)} fusion(f32[32,8,3072]{2,0,1:T(8,128)S(1)} %fusion.32, bf16[1,256,3072]{2,1,0:T(8,128)(2,1)} %copy.45, bf16[7,256,3072]{2,1,0:T(8,128)(2,1)} %reshape.190, bf16[32,512]{1,0:T(8,128)(2,1)S(1)} %convert_element_type.55), kind=kOutput, calls=%fused_computation.5 | convolution fusion | flops 429391872 | bytes 17317888 | tf_op jit(solution)/shard_map/kn,jnp->kjp/dot_general | solution.py:68
  134.8 3.5 %reshape.183 = bf16[16,2,8,3072]{3,1,0,2:T(2,128)(2,1)S(1)} reshape(bf16[32,8,3072]{2,0,1:T(8,128)(2,1)} %fusion.7) | data formatting | bytes 3145728 | tf_op jit(solution)/shard_map/reshape | solution.py:73
  138.3 2.7 %copy.46 = bf16[16,2,8,3072]{3,1,2,0:T(2,128)(2,1)} copy(bf16[16,2,8,3072]{3,1,0,2:T(2,128)(2,1)S(1)} %reshape.183) | data formatting | bytes 3145728 | tf_op jit(solution)/shard_map/reshape | solution.py:73
  141.0 3.7 %all-to-all-start = ((bf16[16,2,8,3072]{3,1,2,0:T(2,128)(2,1)}), bf16[16,2,8,3072]{3,1,2,0:T(2,128)(2,1)S(1)}, u32[]{:S(2)}, u32[]{:S(2)}) async-start(bf16[16,2,8,3072]{3,1,2,0:T(2,128)(2,1)} %copy.46), calls=%async_computation | async-start | bytes 3145728 | tf_op jit(solution)/shard_map/all_to_all | solution.py:72
  144.8 19.0 %all-to-all-done = bf16[16,2,8,3072]{3,1,2,0:T(2,128)(2,1)S(1)} async-done(((bf16[16,2,8,3072]{3,1,2,0:T(2,128)(2,1)}), bf16[16,2,8,3072]{3,1,2,0:T(2,128)(2,1)S(1)}, u32[]{:S(2)}, u32[]{:S(2)}) %all-to-all-start) | async-done | bytes 1572896 | tf_op jit(solution)/shard_map/all_to_all | solution.py:72
  163.8 0.3 copy.47
  164.1 0.6 fusion.11
  164.7 0.6 fusion.16
  165.3 17.0 %all-gather = f32[32,64,64]{2,1,0:T(8,128)S(1)} all-gather(f32[4,64,64]{2,1,0:T(8,128)S(1)} %fusion.16), channel_id=2, replica_groups=mesh['tm'=4,'pts'=8] {'pts'}, dimensions={0}, use_global_device_ids=true | all-gather | bytes 589824 | tf_op jit(solution)/shard_map/all_gather | solution.py:91
  182.5 0.7 multiply_reduce_fusion
  183.1 0.4 fusion.20
  183.5 0.3 fusion.34
  184.1 0.3 fusion.19
  184.4 0.3 fusion.37
  184.6 0.3 fusion.36
  184.9 0.3 fusion.18
  185.4 0.3 fusion.38
  185.7 0.3 fusion.17
  185.9 0.3 convolution_convert_fusion.1
  186.2 1.7 convolution_convert_fusion
  187.9 4.6 %reshape.185 = bf16[4,2,32,3,1024]{4,3,2,1,0:T(4,128)(2,1)S(1)} reshape(bf16[4,64,3072]{2,1,0:T(8,128)(2,1)} %convolution_convert_fusion) | data formatting | bytes 3145728 | tf_op jit(solution)/shard_map/reshape | solution.py:96
  192.5 1.8 copy.49
  (20 shorter events, 1.1 us)
Async XLA Ops:
  0.6 1.4 slice-start
  3.6 121.6 %collective-permute-start = (bf16[256,3,1024]{0,2,1:T(8,128)(2,1)}, bf16[256,3,1024]{0,2,1:T(8,128)(2,1)}, u32[]{:S(2)}, u32[]{:S(2)}) collective-permute-start(bf16[256,3,1024]{0,2,1:T(8,128)(2,1)} %copy.54), channel_id=1, source_target_pairs={{8,0},{16,8},{24,16},{0,24},{9,1},{17,9},{25,17},{1,25},{10,2},{18... | collective-permute-start | bytes 4718600 | tf_op jit(solution)/shard_map/ppermute | solution.py:15
  26.3 10.2 %copy-start.1 = (s32[16]{0:T(128)S(1)}, s32[16]{0:T(128)}, u32[]{:S(2)}) copy-start(s32[16]{0:T(128)} %param.5) | copy-start | bytes 196
  138.3 6.4 %copy-start = (f32[1024]{0:T(1024)S(1)}, f32[1024]{0:T(1024)}, u32[]{:S(2)}) copy-start(f32[1024]{0:T(1024)} %param.4) | copy-start | bytes 12292
  141.0 22.8 %all-to-all-start = ((bf16[16,2,8,3072]{3,1,2,0:T(2,128)(2,1)}), bf16[16,2,8,3072]{3,1,2,0:T(2,128)(2,1)S(1)}, u32[]{:S(2)}, u32[]{:S(2)}) async-start(bf16[16,2,8,3072]{3,1,2,0:T(2,128)(2,1)} %copy.46), calls=%async_computation | async-start | bytes 3145728 | tf_op jit(solution)/shard_map/all_to_all | solution.py:72
